TPU v7x, 256 devices: a whole 4x4x8 slice. The times are simulated.
256 devices in a mesh: dp: 4 (over y), seq: 8 (over x, core), tensor: 8 (over z).
Axes of the slice: x: 4, y: 4, z: 8, core: 2. Of those that a mesh axis runs over, the one named last changes fastest.
Arguments:
- x_in: bfloat16 [4, 4096, 8192], P('dp', 'seq', 'tensor'), may hold values from -0.0625 to 0.0625
- b_in: bfloat16 [4, 4096, 1024], P('dp', 'seq', 'tensor'), may hold values from -3 to 3
- c_in: bfloat16 [4, 4096, 1024], P('dp', 'seq', 'tensor'), may hold values from -3 to 3
- log_decay: float32 [4, 4096, 128], P('dp', 'seq', 'tensor'), may hold values from -1 to 0, as said below
- out_weight: bfloat16 [8192, 4096], P('tensor'), may hold values from -0.0625 to 0.0625
- out_grad: bfloat16 [4, 4096, 4096], P('dp', 'seq', 'tensor'), may hold values from -0.078125 to 0.078125
Outputs:
- weight_grad: bfloat16 [8192, 4096], P('tensor', ('dp', 'seq'))
- x_grad: bfloat16 [4, 4096, 8192], P('dp', 'seq', 'tensor')
- b_grad: bfloat16 [4, 4096, 1024], P('dp', 'seq', 'tensor')
- c_grad: bfloat16 [4, 4096, 1024], P('dp', 'seq', 'tensor')
Inputs may be any that keep to these rules, and one draw needn't show every extreme that they name: `log_decay`: every log-decay is below zero.
All inputs are finite; a program needn't handle non-finite values.
Results may differ from a plain program's by a relative error of at most 0.017.
Values may be sent and summed in bfloat16 or wider, within the bound.
A program may use at most 192 MiB of HBM per device.

v0:
```python
from types import SimpleNamespace

import jax
import jax.numpy as jnp
from jax import lax
from jax.experimental import pallas as pl
from jax.experimental.pallas import tpu as pltpu
from jax.sharding import PartitionSpec as P

F32 = jnp.float32
BF16 = jnp.bfloat16
MESH = pl.DeviceIdType.MESH
NEG = -1e30

VMEM_SCRATCH = dict(
    xv=((512, 1024), BF16),
    bv=((512, 128), BF16),
    cv=((512, 128), BF16),
    dv=((512, 16), F32),
    wv=((8, 1024, 512), BF16),
    cot=((8, 512, 512), BF16),
    cot_sib=((8, 512, 256), BF16),
    b_t=((2, 128, 256), BF16),
    c_t=((2, 128, 256), BF16),
    la=((16, 512, 128), F32),
    la_row=((32, 8, 256), F32),
    tots=((2, 2, 8, 512), F32),
    aff=((2, 256, 256), F32),
    aff_t=((2, 256, 256), F32),
    within_t=((32, 3, 128, 128), BF16),
    weights_t=((32, 3, 128, 128), BF16),
    x_end=((512, 1024), BF16),
    inner=((512, 1024), F32),
    y_acc=((512, 1024), F32),
    gy=((512, 1024), BF16),
    gy_start=((512, 1024), BF16),
    scan_t=((1024, 512), BF16),
    scan_t_sib=((1024, 512), BF16),
    adds=((2, 2, 128, 512), F32),
    loc=((2, 2, 128, 512), F32),
    inc=((2, 2, 128, 512), F32),
    inh=((128, 512), F32),
    ent=((2, 2, 128, 512), BF16),
    lv=((2, 2, 128, 512), BF16),
    l1_out=((2, 2, 128, 512), BF16),
    l1_in=((2, 128, 512), BF16),
    l2_out=((2, 128, 512), BF16),
    l2_in=((2, 3, 128, 512), BF16),
    l3_out=((2, 128, 512), BF16),
    l3_in=((2, 128, 512), BF16),
    d_own=((2, 8, 512), F32),
    d_sib=((8, 512), F32),
    d_chip=((4, 8, 512), F32),
    part=((8, 1024, 256), BF16),
    xa_in=((4, 3, 512, 128), BF16),
    ya_in=((2, 3, 512, 256), BF16),
    xq=((4, 512, 128), BF16),
    yq=((2, 512, 256), BF16),
    xb_in=((3, 512, 128), BF16),
    yb_in=((3, 512, 128), BF16),
    aff_grad=((2, 256, 256), F32),
    x_out=((512, 1024), BF16),
    b_out=((512, 128), BF16),
    c_out=((512, 128), BF16),
    w_out=((1024, 128), BF16),
)
SEMAPHORES = dict(
    load=(6,),
    load_w=(8,),
    right_s=(7,),
    right_r=(7,),
    left_s=(7,),
    left_r=(7,),
    sib_s=(32,),
    sib_r=(32,),
    scan_s=(1,),
    scan_r=(1,),
    ds_s=(1,),
    ds_r=(1,),
    dc_s=(4,),
    dc_r=(4,),
    l1_s=(2,),
    l1_r=(2,),
    l2_s=(6,),
    l2_r=(6,),
    l3_s=(2,),
    l3_r=(2,),
    xa_s=(16,),
    xa_r=(12,),
    ya_s=(8,),
    ya_r=(6,),
    xb_s=(4,),
    xb_r=(3,),
    yb_s=(4,),
    yb_r=(3,),
    store=(4,),
)
NAMES = list(VMEM_SCRATCH) + [f"{n}_sem" for n in SEMAPHORES]


def mm(a, b):
    return jnp.dot(a, b, preferred_element_type=F32)


def mm_nt(a, b):
    return lax.dot_general(a, b, (((1,), (1,)), ((), ())), preferred_element_type=F32)


def at128(i, size=128):
    return pl.ds(pl.multiple_of(i * 128, 128), size)


def at256(i, size=256):
    return pl.ds(pl.multiple_of(i * 256, 256), size)


def split3(v):
    hi = v.astype(BF16)
    rest = v - hi.astype(F32)
    mid = rest.astype(BF16)
    return hi, mid, (rest - mid.astype(F32)).astype(BF16)


def kernel(x_hbm, b_hbm, c_hbm, d_hbm, w_hbm, g_hbm, wg_hbm, xg_hbm, bg_hbm, cg_hbm, *scratch):
    S = SimpleNamespace(**dict(zip(NAMES, scratch)))
    y = lax.axis_index("dp")
    s = lax.axis_index("seq")
    z = lax.axis_index("tensor")
    x = s // 2
    c = s % 2
    sib = (y, x * 2 + (1 - c), z)
    right = (y, s, (z + 1) % 8)
    left = (y, s, (z + 7) % 8)

    def x_peer(xx):
        return (y, xx * 2 + c, z)

    def y_peer(yy):
        return (yy, s, z)

    def remote(src, dst, send_sem, recv_sem, device):
        return pltpu.make_async_remote_copy(
            src_ref=src,
            dst_ref=dst,
            send_sem=send_sem,
            recv_sem=recv_sem,
            device_id=device,
            device_id_type=MESH,
        )

    loads = [
        pltpu.make_async_copy(d_hbm.at[0], S.dv, S.load_sem.at[0]),
        pltpu.make_async_copy(b_hbm.at[0], S.bv, S.load_sem.at[1]),
        pltpu.make_async_copy(c_hbm.at[0], S.cv, S.load_sem.at[2]),
        pltpu.make_async_copy(x_hbm.at[0], S.xv, S.load_sem.at[3]),
        pltpu.make_async_copy(g_hbm.at[0], S.cot.at[z], S.load_sem.at[4]),
    ]
    for load in loads:
        load.start()

    def load_w(k):
        return pltpu.make_async_copy(
            w_hbm.at[:, pl.ds(pl.multiple_of(k * 512, 512), 512)], S.wv.at[k], S.load_w_sem.at[k]
        )

    load_w(z).start()

    barrier = pltpu.get_barrier_semaphore()
    peers = [sib, right, left]
    peers += [x_peer((x + i) % 4) for i in (1, 2, 3)] + [y_peer((y + i) % 4) for i in (1, 2, 3)]
    for peer in peers:
        pl.semaphore_signal(barrier, inc=1, device_id=peer, device_id_type=MESH)
    pl.semaphore_wait(barrier, len(peers))

    def ring(u, k_right, k_left, own=False):
        half_r = u % 2
        half_l = 1 - u % 2
        rows_r = at256(half_r)
        rows_l = at256(half_l)
        src_r = g_hbm.at[0, rows_r] if own else S.cot.at[k_right, rows_r]
        src_l = g_hbm.at[0, rows_l] if own else S.cot.at[k_left, rows_l]
        return (
            remote(src_r, S.cot.at[k_right, rows_r], S.right_s_sem.at[u], S.right_r_sem.at[u], right),
            remote(src_l, S.cot.at[k_left, rows_l], S.left_s_sem.at[u], S.left_r_sem.at[u], left),
        )

    for u in (0, 1):
        for copy in ring(u, z, z, own=True):
            copy.start()

    def start_w(i, carry):
        load_w((z + i) % 8).start()
        return carry

    lax.fori_loop(1, 8, start_w, 0)

    def sib_columns(k, half):
        copies = []
        for j in (0, 1):
            i = k * 4 + half * 2 + j
            copies.append(
                remote(
                    S.cot.at[k, at256(half), at128(2 * j + 1 - c)],
                    S.cot_sib.at[k, at256(half), pl.ds(j * 128, 128)],
                    S.sib_s_sem.at[i],
                    S.sib_r_sem.at[i],
                    sib,
                )
            )
        return copies

    def y_block(k, half, first=False):
        rows = at256(half)

        def tile(n, carry):
            cols = at256(n)
            part = mm_nt(S.cot[k, rows, :], S.wv[k, cols, :])
            if first:
                S.y_acc[rows, cols] = part
            else:
                S.y_acc[rows, cols] += part
            return carry

        lax.fori_loop(0, 4, tile, 0)

    def ring_step(t):
        d = t // 2 + 1
        k_right = (z + 8 - d) % 8
        k_left = (z + d) % 8
        for copy in ring(t, k_right, k_left):
            copy.wait_recv()

        @pl.when(t <= 4)
        def _():
            for copy in ring(t + 2, k_right, k_left):
                copy.start()

        for copy in sib_columns(k_right, t % 2) + sib_columns(k_left, 1 - t % 2):
            copy.start()
        y_block(k_right, t % 2)
        y_block(k_left, 1 - t % 2)

    def iota(shape, dim):
        return lax.broadcasted_iota(jnp.int32, shape, dim)

    low_lanes = iota((256, 128), 1) < 64
    lane_row = iota((1, 128), 1)
    lane_masks = [
        jnp.where(lane_row < 64, 1.0, 0.0).astype(BF16),
        jnp.where(lane_row < 64, 0.0, 1.0).astype(BF16),
    ]
    lower = iota((128, 128), 0) >= iota((128, 128), 1)
    upper = iota((128, 128), 1) >= iota((128, 128), 0)

    loads[0].wait()
    place = jnp.where(iota((16, 128), 0) == iota((16, 128), 1), 1.0, 0.0).astype(BF16)
    tril = jnp.where(iota((256, 256), 0) >= iota((256, 256), 1), 1.0, 0.0).astype(BF16)
    for sp in (0, 1):
        rows = pl.ds(sp * 256, 256)
        padded = sum(mm(p, place) for p in split3(S.dv[rows, :]))
        running = sum(mm(tril, p) for p in split3(padded))
        for h in range(16):
            S.la[h, rows, :] = jnp.broadcast_to(running[:, h : h + 1], (256, 128))
        turned = running.T
        for h in range(16):
            S.la_row[sp * 16 + h] = jnp.broadcast_to(turned[h : h + 1, :], (8, 256))

    def pair_log(rows, hp):
        return jnp.where(low_lanes, S.la[2 * hp, rows, :], S.la[2 * hp + 1, rows, :])

    def where_of(it):
        sp = it // 8
        hp = it % 8
        return sp, hp, at256(sp), at128(hp), hp // 4, at128(hp % 4)

    for load in loads[1:4]:
        load.wait()
    for sp in (0, 1):
        rows = pl.ds(sp * 256, 256)
        S.b_t[sp] = S.bv[rows, :].astype(F32).T.astype(BF16)
        S.c_t[sp] = S.cv[rows, :].astype(F32).T.astype(BF16)

    def span_add(it, carry):
        sp, hp, rows, lanes, half, half_lanes = where_of(it)
        logs = pair_log(rows, hp)
        total = logs[255:256, :]
        S.tots[sp, half, :, half_lanes] = jnp.broadcast_to(total, (8, 128))
        scaled = (jnp.exp(total - logs) * S.xv[rows, lanes].astype(F32)).astype(BF16)
        S.x_end[rows, lanes] = scaled
        S.adds[sp, half, :, half_lanes] = mm(S.b_t[sp], scaled)
        return carry

    lax.fori_loop(0, 16, span_add, 0)

    def row(ref):
        return ref[0:1, :]

    def exchange_1(way):
        for half in (0, 1):
            S.l1_out[way, half] = S.loc[way, half].astype(BF16)
        l1_copy(way).start()

    def l1_copy(way):
        return remote(
            S.l1_out.at[way, 1 - c], S.l1_in.at[way], S.l1_s_sem.at[way], S.l1_r_sem.at[way], sib
        )

    def l2_copy(way, dist):
        to = x + dist if way == 0 else x - dist
        i = way * 3 + dist - 1
        return remote(
            S.l2_out.at[way],
            S.l2_in.at[way, dist - 1],
            S.l2_s_sem.at[i],
            S.l2_r_sem.at[i],
            x_peer(to),
        )

    def l3_copy(way):
        return remote(S.l3_out.at[way], S.l3_in.at[way], S.l3_s_sem.at[way], S.l3_r_sem.at[way], sib)

    def place_of(way):
        return (c, x) if way == 0 else (1 - c, 3 - x)

    def exchange_2(way):
        core, chip = place_of(way)
        l1_copy(way).wait_recv()
        one = jnp.ones((1, 512), F32)
        a = jnp.where(core == 0, jnp.exp(row(S.d_sib)), one)
        b = jnp.where(core == 0, one, jnp.exp(S.d_own[c, 0:1, :]))
        S.l2_out[way] = (a * S.loc[way, c] + b * S.l1_in[way].astype(F32)).astype(BF16)
        for dist in (1, 2, 3):

            @pl.when(chip + dist <= 3)
            def _():
                l2_copy(way, dist).start()

    def exchange_3(way):
        core, chip = place_of(way)
        S.inh[...] = jnp.zeros_like(S.inh)
        near = 3 if way == 0 else 1
        for dist in (1, 2, 3):

            @pl.when(chip >= dist)
            def _():
                l2_copy(way, dist).wait_recv()
                term = S.l2_in[way, dist - 1].astype(F32)
                if dist == 2:
                    term = term * jnp.exp(S.d_chip[near, 0:1, :])
                if dist == 3:
                    term = term * jnp.exp(S.d_chip[near, 0:1, :] + S.d_chip[2, 0:1, :])
                S.inh[...] += term

        into = S.inh[...]
        own = S.loc[way, c] + jnp.exp(S.d_own[c, 0:1, :]) * into
        S.l3_out[way] = jnp.where(core == 0, own, into).astype(BF16)
        l3_copy(way).start()
        other = S.l1_in[way].astype(F32) + jnp.exp(row(S.d_sib)) * into
        S.inc[way, c] = jnp.where(core == 0, into, other)

    def exchange_4(way):
        l3_copy(way).wait_recv()
        S.inc[way, 1 - c] = S.l3_in[way].astype(F32)

    def d_sib_copy():
        return remote(S.d_own.at[1 - c], S.d_sib, S.ds_s_sem.at[0], S.ds_r_sem.at[0], sib)

    def d_chip_copy(dist):
        return remote(
            S.d_chip.at[0],
            S.d_chip.at[4 - dist],
            S.dc_s_sem.at[dist],
            S.dc_r_sem.at[4 - dist],
            x_peer((x + dist) % 4),
        )

    for half in (0, 1):
        S.d_own[half] = S.tots[0, half] + S.tots[1, half]
        S.loc[0, half] = jnp.exp(S.tots[1, half, 0:1, :]) * S.adds[0, half] + S.adds[1, half]
    d_sib_copy().start()
    exchange_1(0)

    loads[4].wait()
    for half in (0, 1):
        for copy in sib_columns(z, half):
            copy.start()
    load_w(z).wait()
    for half in (0, 1):
        y_block(z, half, first=True)

    d_sib_copy().wait_recv()
    S.d_chip[0] = S.d_own[c] + S.d_sib[...]
    for dist in (1, 2, 3):
        d_chip_copy(dist).start()
    exchange_2(0)

    for sp in (0, 1):
        rows = pl.ds(sp * 256, 256)
        S.aff[sp] = mm_nt(S.cv[rows, :], S.bv[rows, :])
        S.aff_t[sp] = mm_nt(S.bv[rows, :], S.cv[rows, :])

    def within_span(it, carry):
        sp, hp, rows, lanes, half, half_lanes = where_of(it)
        values = S.xv[rows, lanes]
        top = jnp.zeros((128, 128), F32)
        bottom = jnp.zeros((128, 128), F32)
        for u in (0, 1):
            col = S.la[2 * hp + u, rows, :]
            line = S.la_row[sp * 16 + 2 * hp + u, 0:1, :]
            tl = jnp.exp(jnp.where(lower, col[:128] - line[:, :128], NEG)) * S.aff[sp, :128, :128]
            bl = jnp.exp(col[128:] - line[:, :128]) * S.aff[sp, 128:, :128]
            br = jnp.exp(jnp.where(lower, col[128:] - line[:, 128:], NEG)) * S.aff[sp, 128:, 128:]
            mine = values * lane_masks[u]
            top += mm(tl.astype(BF16), mine[:128])
            bottom += mm(jnp.concatenate([bl.astype(BF16), br.astype(BF16)], axis=1), mine)
        S.inner[at256(sp, 128), lanes] = top
        S.inner[at128(2 * sp + 1), lanes] = bottom
        return carry

    lax.fori_loop(0, 16, within_span, 0)

    lax.fori_loop(1, 8, lambda i, carry: (load_w((z + i) % 8).wait(), carry)[1], 0)
    for dist in (1, 2, 3):
        d_chip_copy(dist).wait_recv()
    ring_step(0)

    exchange_3(0)
    exchange_4(0)
    for half in (0, 1):
        S.ent[0, half] = S.inc[0, half].astype(BF16)
        S.ent[1, half] = (
            jnp.exp(S.tots[0, half, 0:1, :]) * S.inc[0, half] + S.adds[0, half]
        ).astype(BF16)

    def scan_rows(it, carry):
        sp, hp, rows, lanes, half, half_lanes = where_of(it)
        carried = mm(S.cv[rows, :], S.ent[sp, half, :, half_lanes])
        value = S.inner[rows, lanes] + jnp.exp(pair_log(rows, hp)) * carried
        S.scan_t[lanes, rows] = value.T.astype(BF16)
        return carry

    lax.fori_loop(0, 16, scan_rows, 0)
    scan_copy = remote(S.scan_t, S.scan_t_sib, S.scan_s_sem.at[0], S.scan_r_sem.at[0], sib)
    scan_copy.start()

    def block_of(b):
        d = (b + 1) // 2
        return (z + jnp.where(b % 2 == 1, 8 - d, d)) % 8

    def xa_copy(k, j):
        to = 2 * (k % 2) + j
        slot = (x + 4 - to) % 4 - 1
        return to, remote(
            S.part.at[k, pl.ds(0, 512), pl.ds(j * 128, 128)],
            S.xa_in.at[k // 2, slot],
            S.xa_s_sem.at[k * 2 + j],
            S.xa_r_sem.at[(k // 2) * 3 + slot],
            x_peer(to),
        )

    def ya_copy(k):
        to = k // 2
        slot = (y + 4 - to) % 4 - 1
        return to, remote(
            S.part.at[k, pl.ds(512, 512)],
            S.ya_in.at[k % 2, slot],
            S.ya_s_sem.at[k],
            S.ya_r_sem.at[(k % 2) * 3 + slot],
            y_peer(to),
        )

    def xb_copy(k):
        to = k // 2
        slot = (y + 4 - to) % 4 - 1
        return to, remote(
            S.xq.at[to], S.xb_in.at[slot], S.xb_s_sem.at[to], S.xb_r_sem.at[slot], y_peer(to)
        )

    def yb_copy(k, j):
        to = 2 * (k % 2) + j
        slot = (x + 4 - to) % 4 - 1
        return to, remote(
            S.yq.at[k % 2, :, pl.ds(j * 128, 128)],
            S.yb_in.at[slot],
            S.yb_s_sem.at[to],
            S.yb_r_sem.at[slot],
            x_peer(to),
        )

    def weight_part(b, carry):
        k = block_of(b)
        for half in (0, 1):
            for copy in sib_columns(k, half):
                copy.wait_recv()

        def tile(m, inner_carry):
            rows = at256(m)
            mine = jnp.concatenate(
                [S.cot[k, :, at128(c)], S.cot[k, :, at128(2 + c)]], axis=1
            )
            total = mm(S.scan_t[rows, :], mine) + mm(S.scan_t_sib[rows, :], S.cot_sib[k])
            S.part[k, rows, :] = total.astype(BF16)
            return inner_carry

        lax.fori_loop(0, 4, tile, 0)
        for j in (0, 1):
            to, copy = xa_copy(k, j)
            pl.when(to != x)(copy.start)
        to, copy = ya_copy(k)
        pl.when(to != y)(copy.start)
        return carry

    def wait_in(buffer, sem):
        remote(buffer, buffer, sem, sem, sib).wait_recv()

    def weight_turn(b, carry):
        k = block_of(b)
        yk = k // 2
        kx = k % 2

        @pl.when(x // 2 == kx)
        def _():
            for i in (0, 1, 2):
                wait_in(S.xa_in.at[yk, i], S.xa_r_sem.at[yk * 3 + i])
            total = S.part[k, pl.ds(0, 512), at128(x % 2)].astype(F32)
            for i in (0, 1, 2):
                total = total + S.xa_in[yk, i].astype(F32)
            S.xq[yk] = total.astype(BF16)
            to, copy = xb_copy(k)
            pl.when(to != y)(copy.start)

        @pl.when(yk == y)
        def _():
            for i in (0, 1, 2):
                wait_in(S.ya_in.at[kx, i], S.ya_r_sem.at[kx * 3 + i])
            for j in (0, 1):
                cols = pl.ds(j * 128, 128)
                total = S.part[k, pl.ds(512, 512), cols].astype(F32)
                for i in (0, 1, 2):
                    total = total + S.ya_in[kx, i, :, cols].astype(F32)
                S.yq[kx, :, cols] = total.astype(BF16)
                to, copy = yb_copy(k, j)
                pl.when(to != x)(copy.start)

        return carry

    def turned_weights(it, carry):
        sp, hp, rows, lanes, half, half_lanes = where_of(it)
        for u in (0, 1):
            i = sp * 16 + 2 * hp + u
            col = S.la[2 * hp + u, rows, :]
            line = S.la_row[i, 0:1, :]
            tl = jnp.exp(jnp.where(upper, line[:, :128] - col[:128], NEG))
            tr = jnp.exp(line[:, 128:] - col[:128])
            br = jnp.exp(jnp.where(upper, line[:, 128:] - col[128:], NEG))
            S.within_t[i, 0] = tl.astype(BF16)
            S.within_t[i, 1] = tr.astype(BF16)
            S.within_t[i, 2] = br.astype(BF16)
            S.weights_t[i, 0] = (tl * S.aff_t[sp, :128, :128]).astype(BF16)
            S.weights_t[i, 1] = (tr * S.aff_t[sp, :128, 128:]).astype(BF16)
            S.weights_t[i, 2] = (br * S.aff_t[sp, 128:, 128:]).astype(BF16)
        return carry

    scan_copy.wait_recv()

    def ring_pair(i, carry):
        ring_step(2 * i + 1)
        lax.fori_loop(jnp.where(i == 0, 0, 2 * i + 1), 2 * i + 3, weight_part, 0)
        lax.fori_loop(6 * i, jnp.minimum(6 * i + 6, 16), turned_weights, 0)
        ring_step(2 * i + 2)
        low = jnp.where(i == 0, 0, jnp.where(i == 1, 3, 5))
        high = jnp.where(i == 0, 3, 5)
        lax.fori_loop(low, high, weight_turn, 0)
        return carry

    lax.fori_loop(0, 3, ring_pair, 0)

    def pull(it, carry):
        sp, hp, rows, lanes, half, half_lanes = where_of(it)
        grad = S.y_acc[rows, lanes].astype(BF16)
        S.gy[rows, lanes] = grad
        scaled = (jnp.exp(pair_log(rows, hp)) * grad.astype(F32)).astype(BF16)
        S.gy_start[rows, lanes] = scaled
        S.adds[sp, half, :, half_lanes] = mm(S.c_t[sp], scaled)
        return carry

    lax.fori_loop(0, 16, pull, 0)
    for half in (0, 1):
        S.loc[1, half] = S.adds[0, half] + jnp.exp(S.tots[0, half, 0:1, :]) * S.adds[1, half]
    exchange_1(1)
    weight_part(7, 0)
    exchange_2(1)
    lax.fori_loop(5, 7, weight_turn, 0)

    def within_back(it, carry):
        sp, hp, rows, lanes, half, half_lanes = where_of(it)
        values = S.xv[rows, lanes]
        grads = S.gy[rows, lanes]
        top = jnp.zeros((128, 128), F32)
        bottom = jnp.zeros((128, 128), F32)
        tl = jnp.zeros((128, 128), F32)
        tr = jnp.zeros((128, 128), F32)
        br = jnp.zeros((128, 128), F32)
        for u in (0, 1):
            i = sp * 16 + 2 * hp + u
            mine = values * lane_masks[u]
            grad = grads * lane_masks[u]
            pair_top = mm_nt(mine[:128], grads)
            pair_bottom = mm_nt(mine[128:], grads[128:])
            tl += pair_top[:, :128] * S.within_t[i, 0].astype(F32)
            tr += pair_top[:, 128:] * S.within_t[i, 1].astype(F32)
            br += pair_bottom * S.within_t[i, 2].astype(F32)
            top += mm(jnp.concatenate([S.weights_t[i, 0], S.weights_t[i, 1]], axis=1), grad)
            bottom += mm(S.weights_t[i, 2], grad[128:])
        S.inner[at256(sp, 128), lanes] = top
        S.inner[at128(2 * sp + 1), lanes] = bottom
        S.aff_grad[sp, :128, :128] += tl
        S.aff_grad[sp, :128, 128:] += tr
        S.aff_grad[sp, 128:, 128:] += br
        return carry

    S.aff_grad[...] = jnp.zeros_like(S.aff_grad)
    lax.fori_loop(0, 16, within_back, 0)

    for sp in (0, 1):
        rows = pl.ds(sp * 256, 256)
        grad = mm_nt(S.gy_start[rows, :512], S.ent[sp, 0]) + mm_nt(S.gy_start[rows, 512:], S.ent[sp, 1])
        tl = S.aff_grad[sp, :128, :128].T.astype(BF16)
        tr = S.aff_grad[sp, :128, 128:].T.astype(BF16)
        br = S.aff_grad[sp, 128:, 128:].T.astype(BF16)
        writes = S.bv[rows, :]
        S.c_out[pl.ds(sp * 256, 128), :] = (grad[:128] + mm(tl, writes[:128])).astype(BF16)
        S.c_out[pl.ds(sp * 256 + 128, 128), :] = (
            grad[128:] + mm(jnp.concatenate([tr, br], axis=1), writes)
        ).astype(BF16)
    store_c = pltpu.make_async_copy(S.c_out, cg_hbm.at[0], S.store_sem.at[0])
    store_c.start()

    exchange_3(1)
    weight_turn(7, 0)
    exchange_4(1)
    for half in (0, 1):
        S.lv[1, half] = S.inc[1, half].astype(BF16)
        S.lv[0, half] = (
            S.adds[1, half] + jnp.exp(S.tots[1, half, 0:1, :]) * S.inc[1, half]
        ).astype(BF16)

    def x_final(it, carry):
        sp, hp, rows, lanes, half, half_lanes = where_of(it)
        logs = pair_log(rows, hp)
        to_end = jnp.exp(logs[255:256, :] - logs)
        late = mm(S.bv[rows, :], S.lv[sp, half, :, half_lanes])
        S.x_out[rows, lanes] = (S.inner[rows, lanes] + to_end * late).astype(BF16)
        return carry

    lax.fori_loop(0, 16, x_final, 0)
    store_x = pltpu.make_async_copy(S.x_out, xg_hbm.at[0], S.store_sem.at[1])
    store_x.start()

    for sp in (0, 1):
        rows = pl.ds(sp * 256, 256)
        grad = mm_nt(S.x_end[rows, :512], S.lv[sp, 0]) + mm_nt(S.x_end[rows, 512:], S.lv[sp, 1])
        top = S.aff_grad[sp, :128, :].astype(BF16)
        br = S.aff_grad[sp, 128:, 128:].astype(BF16)
        reads = S.cv[rows, :]
        S.b_out[pl.ds(sp * 256, 128), :] = (grad[:128] + mm(top, reads)).astype(BF16)
        S.b_out[pl.ds(sp * 256 + 128, 128), :] = (grad[128:] + mm(br, reads[128:])).astype(BF16)
    store_b = pltpu.make_async_copy(S.b_out, bg_hbm.at[0], S.store_sem.at[2])
    store_b.start()

    for i in (0, 1, 2):
        wait_in(S.xb_in.at[i], S.xb_r_sem.at[i])
    total = S.xq[y].astype(F32)
    for i in (0, 1, 2):
        total = total + S.xb_in[i].astype(F32)
    S.w_out[pl.ds(0, 512), :] = total.astype(BF16)
    for i in (0, 1, 2):
        wait_in(S.yb_in.at[i], S.yb_r_sem.at[i])
    total = S.yq[x // 2, :, at128(x % 2)].astype(F32)
    for i in (0, 1, 2):
        total = total + S.yb_in[i].astype(F32)
    S.w_out[pl.ds(512, 512), :] = total.astype(BF16)
    store_w = pltpu.make_async_copy(S.w_out, wg_hbm, S.store_sem.at[3])
    store_w.start()

    def ring_sent(u, carry):
        for copy in ring(u, z, z):
            copy.wait_send()
        return carry

    lax.fori_loop(0, 7, ring_sent, 0)

    def block_sent(k, carry):
        for half in (0, 1):
            for copy in sib_columns(k, half):
                copy.wait_send()
        for j in (0, 1):
            to, copy = xa_copy(k, j)
            pl.when(to != x)(copy.wait_send)
        to, copy = ya_copy(k)
        pl.when(to != y)(copy.wait_send)

        @pl.when(x // 2 == k % 2)
        def _():
            to, copy = xb_copy(k)
            pl.when(to != y)(copy.wait_send)

        @pl.when(k // 2 == y)
        def _():
            for j in (0, 1):
                to, copy = yb_copy(k, j)
                pl.when(to != x)(copy.wait_send)

        return carry

    lax.fori_loop(0, 8, block_sent, 0)
    scan_copy.wait_send()
    d_sib_copy().wait_send()
    for dist in (1, 2, 3):
        d_chip_copy(dist).wait_send()
    for way in (0, 1):
        l1_copy(way).wait_send()
        l3_copy(way).wait_send()
        core, chip = place_of(way)
        for dist in (1, 2, 3):

            @pl.when(chip + dist <= 3)
            def _():
                l2_copy(way, dist).wait_send()

    for store in (store_c, store_x, store_b, store_w):
        store.wait()


def per_device(x_in, b_in, c_in, log_decay, out_weight, out_grad):
    out_shape = (
        jax.ShapeDtypeStruct((1024, 128), BF16),
        jax.ShapeDtypeStruct((1, 512, 1024), BF16),
        jax.ShapeDtypeStruct((1, 512, 128), BF16),
        jax.ShapeDtypeStruct((1, 512, 128), BF16),
    )
    scratch = [pltpu.VMEM(shape, dtype) for shape, dtype in VMEM_SCRATCH.values()]
    scratch += [pltpu.SemaphoreType.DMA(shape) for shape in SEMAPHORES.values()]
    return pl.pallas_call(
        kernel,
        out_shape=out_shape,
        in_specs=[pl.BlockSpec(memory_space=pl.ANY)] * 6,
        out_specs=[pl.BlockSpec(memory_space=pl.ANY)] * 4,
        scratch_shapes=scratch,
        compiler_params=pltpu.CompilerParams(
            collective_id=0, has_side_effects=True, vmem_limit_bytes=63 * 2**20
        ),
    )(x_in, b_in, c_in, log_decay, out_weight, out_grad)


def solution(mesh):
    in_specs = (
        P("dp", "seq", "tensor"),
        P("dp", "seq", "tensor"),
        P("dp", "seq", "tensor"),
        P("dp", "seq", "tensor"),
        P("tensor", None),
        P("dp", "seq", "tensor"),
    )
    out_specs = (
        P("tensor", ("dp", "seq")),
        P("dp", "seq", "tensor"),
        P("dp", "seq", "tensor"),
        P("dp", "seq", "tensor"),
    )
    return jax.shard_map(
        per_device, mesh=mesh, in_specs=in_specs, out_specs=out_specs, check_vma=False
    )
```

profile of v0, /device:TPU:16, one launch (start us, length us, event | category | flops | bytes accessed | tf_op | source)
XLA Modules:
  0.0 119.3 jit_solution(4591062077678805237)
XLA Ops:
  0.6 1.6 %copy.10.d_hbm = f32[1,512,16]{2,1,0:T(8,128)} copy(f32[1,512,16]{1,2,0:T(8,128)} %param.9) | data formatting | bytes 65536 | tf_op args[3]
  2.2 110.0 %shard_map.93 = (bf16[1024,128]{1,0:T(8,128)(2,1)}, bf16[1,512,1024]{2,1,0:T(8,128)(2,1)}, bf16[1,512,128]{2,1,0:T(8,128)(2,1)}, bf16[1,512,128]{2,1,0:T(8,128)(2,1)}) custom-call(bf16[1,512,1024]{2,1,0:T(8,128)(2,1)} %x_hbm.1, bf16[1,512,128]{2,1,0:T(8,128)(2,1)} %b_hbm.1, bf16[1,512,128]{2,1,0:T(8,128)(2,1)} %c_hbm.1, f32[1,512,16]{2,1,0:T(8,128)} %copy.10.d_hbm, ...), custom_call_target="tpu_custom_call" | custom-call | tf_op jit(solution)/shard_map/pallas_call | solution.py:744
  112.2 1.7 %copy.15 = bf16[1024,128]{1,0:T(8,128)(2,1)} copy(bf16[1024,128]{1,0:T(8,128)(2,1)} %get-tuple-element.8) | data formatting | bytes 524288
  113.9 2.3 %copy.16 = bf16[1,512,1024]{2,1,0:T(8,128)(2,1)} copy(bf16[1,512,1024]{2,1,0:T(8,128)(2,1)} %get-tuple-element.9) | data formatting | bytes 2097152
  116.1 1.6 %copy.17 = bf16[1,512,128]{2,1,0:T(8,128)(2,1)} copy(bf16[1,512,128]{2,1,0:T(8,128)(2,1)} %get-tuple-element.10) | data formatting | bytes 262144
  117.7 1.6 %copy.18 = bf16[1,512,128]{2,1,0:T(8,128)(2,1)} copy(bf16[1,512,128]{2,1,0:T(8,128)(2,1)} %get-tuple-element.11) | data formatting | bytes 262144
where the time goes:
time: 120 us; the launch traced here: 119 us
  Pallas kernels  110 us (92%)
  local copies, waits for them, and re-layouts  8.66 us (7%)
    pallas_call x1, Pallas kernels, per_device(): pl.pallas_call(kernel, out_shape=out_shape, in_specs=[pl.BlockSpec(memory...  110 us
    unnamed x5, local copies, waits for them, and re-layouts  8.66 us

commit v1 on v0

--- a/solution.py
+++ b/solution.py
@@ -11,12 +11,14 @@
 BF16 = jnp.bfloat16
 MESH = pl.DeviceIdType.MESH
 NEG = -1e30
+X_ROWS = 640
+Y_ROWS = 1024 - X_ROWS
 
 VMEM_SCRATCH = dict(
     xv=((512, 1024), BF16),
     bv=((512, 128), BF16),
     cv=((512, 128), BF16),
-    dv=((512, 16), F32),
+    dv=((128, 512), F32),
     wv=((8, 1024, 512), BF16),
     cot=((8, 512, 512), BF16),
     cot_sib=((8, 512, 256), BF16),
@@ -52,12 +54,12 @@
     d_sib=((8, 512), F32),
     d_chip=((4, 8, 512), F32),
     part=((8, 1024, 256), BF16),
-    xa_in=((4, 3, 512, 128), BF16),
-    ya_in=((2, 3, 512, 256), BF16),
-    xq=((4, 512, 128), BF16),
-    yq=((2, 512, 256), BF16),
-    xb_in=((3, 512, 128), BF16),
-    yb_in=((3, 512, 128), BF16),
+    xa_in=((4, 3, X_ROWS, 128), BF16),
+    ya_in=((2, 3, Y_ROWS, 256), BF16),
+    xq=((4, X_ROWS, 128), BF16),
+    yq=((2, Y_ROWS, 256), BF16),
+    xb_in=((3, X_ROWS, 128), BF16),
+    yb_in=((3, Y_ROWS, 128), BF16),
     aff_grad=((2, 256, 256), F32),
     x_out=((512, 1024), BF16),
     b_out=((512, 128), BF16),
@@ -149,7 +151,7 @@
         )
 
     loads = [
-        pltpu.make_async_copy(d_hbm.at[0], S.dv, S.load_sem.at[0]),
+        pltpu.make_async_copy(d_hbm.at[0], S.dv.at[pl.ds(0, 16)], S.load_sem.at[0]),
         pltpu.make_async_copy(b_hbm.at[0], S.bv, S.load_sem.at[1]),
         pltpu.make_async_copy(c_hbm.at[0], S.cv, S.load_sem.at[2]),
         pltpu.make_async_copy(x_hbm.at[0], S.xv, S.load_sem.at[3]),
@@ -212,16 +214,13 @@
     def y_block(k, half, first=False):
         rows = at256(half)
 
-        def tile(n, carry):
-            cols = at256(n)
+        for n in range(4):
+            cols = pl.ds(n * 256, 256)
             part = mm_nt(S.cot[k, rows, :], S.wv[k, cols, :])
             if first:
                 S.y_acc[rows, cols] = part
             else:
                 S.y_acc[rows, cols] += part
-            return carry
-
-        lax.fori_loop(0, 4, tile, 0)
 
     def ring_step(t):
         d = t // 2 + 1
@@ -252,16 +251,16 @@
     lower = iota((128, 128), 0) >= iota((128, 128), 1)
     upper = iota((128, 128), 1) >= iota((128, 128), 0)
 
+    S.dv[16:, :] = jnp.zeros((112, 512), F32)
     loads[0].wait()
-    place = jnp.where(iota((16, 128), 0) == iota((16, 128), 1), 1.0, 0.0).astype(BF16)
     tril = jnp.where(iota((256, 256), 0) >= iota((256, 256), 1), 1.0, 0.0).astype(BF16)
     for sp in (0, 1):
         rows = pl.ds(sp * 256, 256)
-        padded = sum(mm(p, place) for p in split3(S.dv[rows, :]))
-        running = sum(mm(tril, p) for p in split3(padded))
+        parts = split3(S.dv[:, rows])
+        running = sum(mm_nt(tril, p) for p in parts)
         for h in range(16):
             S.la[h, rows, :] = jnp.broadcast_to(running[:, h : h + 1], (256, 128))
-        turned = running.T
+        turned = sum(mm_nt(p[:16], tril) for p in parts)
         for h in range(16):
             S.la_row[sp * 16 + h] = jnp.broadcast_to(turned[h : h + 1, :], (8, 256))
 
@@ -290,7 +289,7 @@
         S.adds[sp, half, :, half_lanes] = mm(S.b_t[sp], scaled)
         return carry
 
-    lax.fori_loop(0, 16, span_add, 0)
+    lax.fori_loop(0, 16, span_add, 0, unroll=8)
 
     def row(ref):
         return ref[0:1, :]
@@ -417,7 +416,7 @@
         S.inner[at128(2 * sp + 1), lanes] = bottom
         return carry
 
-    lax.fori_loop(0, 16, within_span, 0)
+    lax.fori_loop(0, 16, within_span, 0, unroll=8)
 
     lax.fori_loop(1, 8, lambda i, carry: (load_w((z + i) % 8).wait(), carry)[1], 0)
     for dist in (1, 2, 3):
@@ -439,7 +438,7 @@
         S.scan_t[lanes, rows] = value.T.astype(BF16)
         return carry
 
-    lax.fori_loop(0, 16, scan_rows, 0)
+    lax.fori_loop(0, 16, scan_rows, 0, unroll=8)
     scan_copy = remote(S.scan_t, S.scan_t_sib, S.scan_s_sem.at[0], S.scan_r_sem.at[0], sib)
     scan_copy.start()
 
@@ -451,7 +450,7 @@
         to = 2 * (k % 2) + j
         slot = (x + 4 - to) % 4 - 1
         return to, remote(
-            S.part.at[k, pl.ds(0, 512), pl.ds(j * 128, 128)],
+            S.part.at[k, pl.ds(0, X_ROWS), pl.ds(j * 128, 128)],
             S.xa_in.at[k // 2, slot],
             S.xa_s_sem.at[k * 2 + j],
             S.xa_r_sem.at[(k // 2) * 3 + slot],
@@ -462,7 +461,7 @@
         to = k // 2
         slot = (y + 4 - to) % 4 - 1
         return to, remote(
-            S.part.at[k, pl.ds(512, 512)],
+            S.part.at[k, pl.ds(X_ROWS, Y_ROWS)],
             S.ya_in.at[k % 2, slot],
             S.ya_s_sem.at[k],
             S.ya_r_sem.at[(k % 2) * 3 + slot],
@@ -493,16 +492,13 @@
             for copy in sib_columns(k, half):
                 copy.wait_recv()
 
-        def tile(m, inner_carry):
-            rows = at256(m)
+        for m in range(4):
+            rows = pl.ds(m * 256, 256)
             mine = jnp.concatenate(
                 [S.cot[k, :, at128(c)], S.cot[k, :, at128(2 + c)]], axis=1
             )
             total = mm(S.scan_t[rows, :], mine) + mm(S.scan_t_sib[rows, :], S.cot_sib[k])
             S.part[k, rows, :] = total.astype(BF16)
-            return inner_carry
-
-        lax.fori_loop(0, 4, tile, 0)
         for j in (0, 1):
             to, copy = xa_copy(k, j)
             pl.when(to != x)(copy.start)
@@ -522,7 +518,7 @@
         def _():
             for i in (0, 1, 2):
                 wait_in(S.xa_in.at[yk, i], S.xa_r_sem.at[yk * 3 + i])
-            total = S.part[k, pl.ds(0, 512), at128(x % 2)].astype(F32)
+            total = S.part[k, pl.ds(0, X_ROWS), at128(x % 2)].astype(F32)
             for i in (0, 1, 2):
                 total = total + S.xa_in[yk, i].astype(F32)
             S.xq[yk] = total.astype(BF16)
@@ -535,7 +531,7 @@
                 wait_in(S.ya_in.at[kx, i], S.ya_r_sem.at[kx * 3 + i])
             for j in (0, 1):
                 cols = pl.ds(j * 128, 128)
-                total = S.part[k, pl.ds(512, 512), cols].astype(F32)
+                total = S.part[k, pl.ds(X_ROWS, Y_ROWS), cols].astype(F32)
                 for i in (0, 1, 2):
                     total = total + S.ya_in[kx, i, :, cols].astype(F32)
                 S.yq[kx, :, cols] = total.astype(BF16)
@@ -567,10 +563,9 @@
         ring_step(2 * i + 1)
         lax.fori_loop(jnp.where(i == 0, 0, 2 * i + 1), 2 * i + 3, weight_part, 0)
         lax.fori_loop(6 * i, jnp.minimum(6 * i + 6, 16), turned_weights, 0)
+        lax.fori_loop(1, jnp.where(i == 2, 3, 1), weight_turn, 0)
         ring_step(2 * i + 2)
-        low = jnp.where(i == 0, 0, jnp.where(i == 1, 3, 5))
-        high = jnp.where(i == 0, 3, 5)
-        lax.fori_loop(low, high, weight_turn, 0)
+        lax.fori_loop(0, jnp.where(i == 1, 1, 0), weight_turn, 0)
         return carry
 
     lax.fori_loop(0, 3, ring_pair, 0)
@@ -584,13 +579,13 @@
         S.adds[sp, half, :, half_lanes] = mm(S.c_t[sp], scaled)
         return carry
 
-    lax.fori_loop(0, 16, pull, 0)
+    lax.fori_loop(0, 16, pull, 0, unroll=8)
     for half in (0, 1):
         S.loc[1, half] = S.adds[0, half] + jnp.exp(S.tots[0, half, 0:1, :]) * S.adds[1, half]
     exchange_1(1)
     weight_part(7, 0)
     exchange_2(1)
-    lax.fori_loop(5, 7, weight_turn, 0)
+    lax.fori_loop(3, 5, weight_turn, 0)
 
     def within_back(it, carry):
         sp, hp, rows, lanes, half, half_lanes = where_of(it)
@@ -620,7 +615,7 @@
         return carry
 
     S.aff_grad[...] = jnp.zeros_like(S.aff_grad)
-    lax.fori_loop(0, 16, within_back, 0)
+    lax.fori_loop(0, 16, within_back, 0, unroll=8)
 
     for sp in (0, 1):
         rows = pl.ds(sp * 256, 256)
@@ -636,6 +631,7 @@
     store_c = pltpu.make_async_copy(S.c_out, cg_hbm.at[0], S.store_sem.at[0])
     store_c.start()
 
+    lax.fori_loop(5, 7, weight_turn, 0)
     exchange_3(1)
     weight_turn(7, 0)
     exchange_4(1)
@@ -653,7 +649,7 @@
         S.x_out[rows, lanes] = (S.inner[rows, lanes] + to_end * late).astype(BF16)
         return carry
 
-    lax.fori_loop(0, 16, x_final, 0)
+    lax.fori_loop(0, 16, x_final, 0, unroll=8)
     store_x = pltpu.make_async_copy(S.x_out, xg_hbm.at[0], S.store_sem.at[1])
     store_x.start()
 
@@ -673,13 +669,13 @@
     total = S.xq[y].astype(F32)
     for i in (0, 1, 2):
         total = total + S.xb_in[i].astype(F32)
-    S.w_out[pl.ds(0, 512), :] = total.astype(BF16)
+    S.w_out[pl.ds(0, X_ROWS), :] = total.astype(BF16)
     for i in (0, 1, 2):
         wait_in(S.yb_in.at[i], S.yb_r_sem.at[i])
     total = S.yq[x // 2, :, at128(x % 2)].astype(F32)
     for i in (0, 1, 2):
         total = total + S.yb_in[i].astype(F32)
-    S.w_out[pl.ds(512, 512), :] = total.astype(BF16)
+    S.w_out[pl.ds(X_ROWS, Y_ROWS), :] = total.astype(BF16)
     store_w = pltpu.make_async_copy(S.w_out, wg_hbm, S.store_sem.at[3])
     store_w.start()
 
@@ -732,6 +728,30 @@
         store.wait()
 
 
+def copy_kernel(*refs):
+    ins, outs, held, sems = refs[:4], refs[4:8], refs[8:12], refs[12]
+    pieces = []
+    for n, (src, dst, mid) in enumerate(zip(ins, outs, held)):
+        size = 256 if n else 512
+        for i in range(1024 // size if n == 0 else 512 // size):
+            rows = pl.ds(i * size, size)
+            at = (rows,) if n == 0 else (0, rows)
+            j = 2 * len(pieces)
+            pieces.append(
+                (
+                    pltpu.make_async_copy(src.at[at], mid.at[at], sems.at[j]),
+                    pltpu.make_async_copy(mid.at[at], dst.at[at], sems.at[j + 1]),
+                )
+            )
+    for come, _ in pieces:
+        come.start()
+    for come, go in pieces:
+        come.wait()
+        go.start()
+    for _, go in pieces:
+        go.wait()
+
+
 def per_device(x_in, b_in, c_in, log_decay, out_weight, out_grad):
     out_shape = (
         jax.ShapeDtypeStruct((1024, 128), BF16),
@@ -741,7 +761,7 @@
     )
     scratch = [pltpu.VMEM(shape, dtype) for shape, dtype in VMEM_SCRATCH.values()]
     scratch += [pltpu.SemaphoreType.DMA(shape) for shape in SEMAPHORES.values()]
-    return pl.pallas_call(
+    results = pl.pallas_call(
         kernel,
         out_shape=out_shape,
         in_specs=[pl.BlockSpec(memory_space=pl.ANY)] * 6,
@@ -750,7 +770,15 @@
         compiler_params=pltpu.CompilerParams(
             collective_id=0, has_side_effects=True, vmem_limit_bytes=63 * 2**20
         ),
-    )(x_in, b_in, c_in, log_decay, out_weight, out_grad)
+    )(x_in, b_in, c_in, jnp.transpose(log_decay, (0, 2, 1)), out_weight, out_grad)
+    return pl.pallas_call(
+        copy_kernel,
+        out_shape=out_shape,
+        in_specs=[pl.BlockSpec(memory_space=pl.ANY)] * 4,
+        out_specs=[pl.BlockSpec(memory_space=pl.ANY)] * 4,
+        scratch_shapes=[pltpu.VMEM(o.shape, o.dtype) for o in out_shape]
+        + [pltpu.SemaphoreType.DMA((16,))],
+    )(*results)
 
 
 def solution(mesh):

time: 120 us -> 82.6 us (0.69)
  Pallas kernels: 110 us -> 81.8 us
  local copies, waits for them, and re-layouts: 8.66 us -> 0 us
    pallas_call x1, Pallas kernels: 110 us -> 79.5 us  [per_device(): pl.pallas_call(kernel, out_shape=out_shape, in_specs=[pl.BlockSpec(memory...]
    unnamed x5 -> x0, local copies, waits for them, and re-layouts: 8.66 us -> none
    pallas_call x0 -> x1, Pallas kernels: none -> 2.36 us  [per_device(): pl.pallas_call(copy_kernel, out_shape=out_shape, in_specs=[pl.BlockSpec(m...]
where the time goes in v1:
time: 82.6 us; the launch traced here: 82.5 us
  Pallas kernels  81.8 us (99%)
    pallas_call x1, Pallas kernels, per_device(): pl.pallas_call(kernel, out_shape=out_shape, in_specs=[pl.BlockSpec(memory...  79.5 us
    pallas_call x1, Pallas kernels, per_device(): pl.pallas_call(copy_kernel, out_shape=out_shape, in_specs=[pl.BlockSpec(m...  2.36 us

profile of v1, /device:TPU:16, one launch (start us, length us, event | category | flops | bytes accessed | tf_op | source)
XLA Modules:
  0.0 82.5 jit_solution(2376104302669768484)
XLA Ops:
  0.6 79.5 %shard_map.93 = (bf16[1024,128]{1,0:T(8,128)(2,1)}, bf16[1,512,1024]{2,1,0:T(8,128)(2,1)}, bf16[1,512,128]{2,1,0:T(8,128)(2,1)}, bf16[1,512,128]{2,1,0:T(8,128)(2,1)}) custom-call(bf16[1,512,1024]{2,1,0:T(8,128)(2,1)} %x_hbm.1, bf16[1,512,128]{2,1,0:T(8,128)(2,1)} %b_hbm.1, bf16[1,512,128]{2,1,0:T(8,128)(2,1)} %c_hbm.1, f32[1,16,512]{2,1,0:T(8,128)} %bitcast.1, ...), custom_call_target="tpu_custom_call" | custom-call | tf_op jit(solution)/shard_map/pallas_call | solution.py:764
  80.1 2.4 %shard_map.94 = (bf16[1024,128]{1,0:T(8,128)(2,1)}, bf16[1,512,1024]{2,1,0:T(8,128)(2,1)}, bf16[1,512,128]{2,1,0:T(8,128)(2,1)}, bf16[1,512,128]{2,1,0:T(8,128)(2,1)}) custom-call(bf16[1024,128]{1,0:T(8,128)(2,1)} %get-tuple-element.8.refs_0_, bf16[1,512,1024]{2,1,0:T(8,128)(2,1)} %get-tuple-element.9.refs_1_, ...), custom_call_target="tpu_custom_call" | custom-call | tf_op jit(solution)/shard_map/pallas_call | solution.py:774

commit v2 on v1

--- a/solution.py
+++ b/solution.py
@@ -11,7 +11,7 @@
 BF16 = jnp.bfloat16
 MESH = pl.DeviceIdType.MESH
 NEG = -1e30
-X_ROWS = 640
+X_ROWS = 608
 Y_ROWS = 1024 - X_ROWS
 
 VMEM_SCRATCH = dict(
@@ -424,6 +424,7 @@
     ring_step(0)
 
     exchange_3(0)
+    ring_step(1)
     exchange_4(0)
     for half in (0, 1):
         S.ent[0, half] = S.inc[0, half].astype(BF16)
@@ -560,7 +561,7 @@
     scan_copy.wait_recv()
 
     def ring_pair(i, carry):
-        ring_step(2 * i + 1)
+        pl.when(i > 0)(lambda: ring_step(2 * i + 1))
         lax.fori_loop(jnp.where(i == 0, 0, 2 * i + 1), 2 * i + 3, weight_part, 0)
         lax.fori_loop(6 * i, jnp.minimum(6 * i + 6, 16), turned_weights, 0)
         lax.fori_loop(1, jnp.where(i == 2, 3, 1), weight_turn, 0)

time: 82.6 us -> 82.3 us (level)
  no operation moved by 1% of the time
where the time goes in v2:
time: 82.3 us; the launch traced here: 82.2 us
  Pallas kernels  81.6 us (99%)
    pallas_call x1, Pallas kernels, per_device(): pl.pallas_call(kernel, out_shape=out_shape, in_specs=[pl.BlockSpec(memory...  79.2 us
    pallas_call x1, Pallas kernels, per_device(): pl.pallas_call(copy_kernel, out_shape=out_shape, in_specs=[pl.BlockSpec(m...  2.36 us

profile of v2, /device:TPU:16, one launch (start us, length us, event | category | flops | bytes accessed | tf_op | source)
XLA Modules:
  0.0 82.2 jit_solution(4771936839609394532)
XLA Ops:
  0.6 79.2 %shard_map.93 = (bf16[1024,128]{1,0:T(8,128)(2,1)}, bf16[1,512,1024]{2,1,0:T(8,128)(2,1)}, bf16[1,512,128]{2,1,0:T(8,128)(2,1)}, bf16[1,512,128]{2,1,0:T(8,128)(2,1)}) custom-call(bf16[1,512,1024]{2,1,0:T(8,128)(2,1)} %x_hbm.1, bf16[1,512,128]{2,1,0:T(8,128)(2,1)} %b_hbm.1, bf16[1,512,128]{2,1,0:T(8,128)(2,1)} %c_hbm.1, f32[1,16,512]{2,1,0:T(8,128)} %bitcast.1, ...), custom_call_target="tpu_custom_call" | custom-call | tf_op jit(solution)/shard_map/pallas_call | solution.py:765
  79.9 2.4 %shard_map.94 = (bf16[1024,128]{1,0:T(8,128)(2,1)}, bf16[1,512,1024]{2,1,0:T(8,128)(2,1)}, bf16[1,512,128]{2,1,0:T(8,128)(2,1)}, bf16[1,512,128]{2,1,0:T(8,128)(2,1)}) custom-call(bf16[1024,128]{1,0:T(8,128)(2,1)} %get-tuple-element.8.refs_0_, bf16[1,512,1024]{2,1,0:T(8,128)(2,1)} %get-tuple-element.9.refs_1_, ...), custom_call_target="tpu_custom_call" | custom-call | tf_op jit(solution)/shard_map/pallas_call | solution.py:775

commit v3 on v2

--- a/solution.py
+++ b/solution.py
@@ -732,9 +732,9 @@
 def copy_kernel(*refs):
     ins, outs, held, sems = refs[:4], refs[4:8], refs[8:12], refs[12]
     pieces = []
-    for n, (src, dst, mid) in enumerate(zip(ins, outs, held)):
-        size = 256 if n else 512
-        for i in range(1024 // size if n == 0 else 512 // size):
+    for n, size, count in ((1, 64, 8), (0, 256, 4), (2, 512, 1), (3, 512, 1)):
+        src, dst, mid = ins[n], outs[n], held[n]
+        for i in range(count):
             rows = pl.ds(i * size, size)
             at = (rows,) if n == 0 else (0, rows)
             j = 2 * len(pieces)
@@ -778,7 +778,7 @@
         in_specs=[pl.BlockSpec(memory_space=pl.ANY)] * 4,
         out_specs=[pl.BlockSpec(memory_space=pl.ANY)] * 4,
         scratch_shapes=[pltpu.VMEM(o.shape, o.dtype) for o in out_shape]
-        + [pltpu.SemaphoreType.DMA((16,))],
+        + [pltpu.SemaphoreType.DMA((28,))],
     )(*results)
 
 

time: 82.3 us -> 82.3 us (level)
  no operation moved by 1% of the time
where the time goes in v3:
time: 82.3 us; the launch traced here: 82.2 us
  Pallas kernels  81.6 us (99%)
    pallas_call x1, Pallas kernels, per_device(): pl.pallas_call(kernel, out_shape=out_shape, in_specs=[pl.BlockSpec(memory...  79.2 us
    pallas_call x1, Pallas kernels, per_device(): pl.pallas_call(copy_kernel, out_shape=out_shape, in_specs=[pl.BlockSpec(m...  2.37 us

profile of v3, /device:TPU:16, one launch (start us, length us, event | category | flops | bytes accessed | tf_op | source)
XLA Modules:
  0.0 82.2 jit_solution(13012390509894011863)
XLA Ops:
  0.6 79.2 %shard_map.93 = (bf16[1024,128]{1,0:T(8,128)(2,1)}, bf16[1,512,1024]{2,1,0:T(8,128)(2,1)}, bf16[1,512,128]{2,1,0:T(8,128)(2,1)}, bf16[1,512,128]{2,1,0:T(8,128)(2,1)}) custom-call(bf16[1,512,1024]{2,1,0:T(8,128)(2,1)} %x_hbm.1, bf16[1,512,128]{2,1,0:T(8,128)(2,1)} %b_hbm.1, bf16[1,512,128]{2,1,0:T(8,128)(2,1)} %c_hbm.1, f32[1,16,512]{2,1,0:T(8,128)} %bitcast.1, ...), custom_call_target="tpu_custom_call" | custom-call | tf_op jit(solution)/shard_map/pallas_call | solution.py:765
  79.9 2.4 %shard_map.94 = (bf16[1024,128]{1,0:T(8,128)(2,1)}, bf16[1,512,1024]{2,1,0:T(8,128)(2,1)}, bf16[1,512,128]{2,1,0:T(8,128)(2,1)}, bf16[1,512,128]{2,1,0:T(8,128)(2,1)}) custom-call(bf16[1024,128]{1,0:T(8,128)(2,1)} %get-tuple-element.8.refs_0_, bf16[1,512,1024]{2,1,0:T(8,128)(2,1)} %get-tuple-element.9.refs_1_, ...), custom_call_target="tpu_custom_call" | custom-call | tf_op jit(solution)/shard_map/pallas_call | solution.py:775
